TPU v7x, 32 devices: a whole 2x2x4 slice. The times are simulated.
32 devices in a mesh: band: 2 (over core), grow: 4 (over z), gcol: 4 (over y, x).
Axes of the slice: x: 2, y: 2, z: 4, core: 2. Of those that a mesh axis runs over, the one named last changes fastest.
Arguments:
- valence_orbitals: bfloat16 [16, 98304], replicated, may hold values from -6 to 6
- conduction_orbitals: bfloat16 [128, 98304], P(('band', 'grow', 'gcol')), may hold values from -6 to 6
- valence_energy: float32 [16], replicated, may hold values from -3 to -0.5
- conduction_energy: float32 [128], replicated, may hold values from 0.5 to 3
- coulomb_root: float32 [12288], replicated, may hold values from 0.2 to 2
- pair_bands: int32 [2, 640], P(None, ('band', 'grow', 'gcol')), may hold values from 0 to 127, as said below
- slot_counts: int32 [32], P(('band', 'grow', 'gcol')), may hold values from 1 to 19, as said below
Outputs:
- chi_zero: float32 [2, 12288, 12288], P('band', 'grow', 'gcol')
Inputs may be any that keep to these rules, and one draw needn't show every extreme that they name: `pair_bands`: the slots of device d name conduction orbitals d * 4 to (d + 1) * 4 - 1 only, each of them at least once; no (valence, conduction) pair appears in two slots anywhere. `slot_counts`: the two devices of one chip (same grow and gcol index, band 0 and band 1) hold at most 20 live slots together; some chip holds exactly 20, and some device holds exactly 19.
All inputs are finite; a program needn't handle non-finite values.
Results may differ from a plain program's by a relative error of at most 0.012.
Values may be sent and summed in bfloat16 or wider, within the bound.
A program may use at most 128 MiB of HBM per device.

v0:
```python
import math

import jax
import jax.numpy as jnp
from jax import lax
from jax.sharding import PartitionSpec as P

N1 = 16
N2 = 24
N3 = 32
M1 = 32
M2 = 48
M3 = 64
SLOTS = 20
FREQS = 2


def pruned_table(keep, length):
    rows_i = lax.broadcasted_iota(jnp.int32, (keep, length), 0)
    cols_i = lax.broadcasted_iota(jnp.int32, (keep, length), 1)
    wave = (rows_i - keep // 2) % length
    angles = (wave * cols_i % length).astype(jnp.float32) * (2.0 * math.pi / length)
    return (jnp.cos(angles) + jnp.sin(angles)) / math.sqrt(length)


def densities(valence_orbitals, con_table, coulomb_root, val_index, con_local):
    highest = lax.Precision.HIGHEST
    count_slots = val_index.shape[0]
    products = valence_orbitals[val_index].astype(jnp.float32) * con_table[con_local].astype(
        jnp.float32
    )
    lattice = products.reshape(count_slots, M1, M2, M3)
    lattice = jnp.einsum("pabc,kc->pabk", lattice, pruned_table(N3, M3), precision=highest)
    lattice = jnp.einsum("pabc,kb->pakc", lattice, pruned_table(N2, M2), precision=highest)
    lattice = jnp.einsum("pabc,ka->pkbc", lattice, pruned_table(N1, M1), precision=highest)
    return (lattice.reshape(count_slots, N1 * N2 * N3) * coulomb_root).astype(jnp.bfloat16)


def weights_of(valence_energy, conduction_energy, val_index, con_index, is_live, factor):
    energy_gap = conduction_energy[con_index] - valence_energy[val_index]
    frequency = jnp.arange(FREQS).astype(jnp.float32)[:, None]
    response = 2.0 * energy_gap / (energy_gap * energy_gap + frequency * frequency)
    return jnp.where(is_live, response, 0.0) * factor


def per_device(
    valence_orbitals,
    conduction_orbitals,
    valence_energy,
    conduction_energy,
    coulomb_root,
    pair_bands,
    slot_counts,
):
    grow_size = lax.axis_size("grow")
    gcol_size = lax.axis_size("gcol")
    all_devices = lax.axis_size("band") * grow_size * gcol_size
    factor = 1.0 / math.sqrt(all_devices * SLOTS)
    local_slots = pair_bands.shape[1]
    held_con = conduction_orbitals.shape[0]
    both_lists, both_counts, both_con = (
        lax.all_gather(pair_bands, "band", axis=1, tiled=True),
        lax.all_gather(slot_counts, "band", axis=0, tiled=True),
        lax.all_gather(conduction_orbitals, "band", axis=0, tiled=True),
    )
    half_slots = local_slots // 2
    band_rank = lax.axis_index("band")
    position = band_rank * half_slots + jnp.arange(half_slots)
    first_count = both_counts[0]
    source = jnp.where(position < first_count, position, local_slots + position - first_count)
    source = jnp.minimum(source, 2 * local_slots - 1)
    is_live = position < first_count + both_counts[1]
    val_index = both_lists[0][source]
    con_index = both_lists[1][source]
    con_local = con_index % held_con + source // local_slots * held_con
    density = densities(valence_orbitals, both_con, coulomb_root, val_index, con_local)
    pair_weight = weights_of(
        valence_energy, conduction_energy, val_index, con_index, is_live, factor
    )
    count_slots = density.shape[0]
    total_planes = density.shape[1]
    row_block = total_planes // grow_size
    col_block = total_planes // gcol_size
    results = []
    row_panel = lax.all_to_all(
        density.reshape(count_slots, grow_size, row_block),
        "grow",
        split_axis=1,
        concat_axis=0,
        tiled=True,
    )
    row_panel = lax.all_gather(row_panel, "gcol", axis=0, tiled=True)
    col_panel = lax.all_to_all(
        density.reshape(count_slots, gcol_size, col_block),
        "gcol",
        split_axis=1,
        concat_axis=0,
        tiled=True,
    )
    col_panel = lax.all_gather(col_panel, "grow", axis=0, tiled=True)
    weight_all = lax.all_gather(pair_weight, ("grow", "gcol"), axis=1, tiled=True)
    row_four = row_panel.reshape(gcol_size, grow_size, count_slots, row_block)
    col_four = col_panel.reshape(grow_size, gcol_size, count_slots, col_block)
    weight_four = weight_all.reshape(FREQS, grow_size, gcol_size, count_slots)
    for which in range(FREQS):
        weighted = (col_four * weight_four[which][:, :, :, None]).astype(jnp.bfloat16)
        results.append(
            jnp.einsum("crsi,rcsj->ij", row_four, weighted, preferred_element_type=jnp.float32)
        )
    chi_parts = jnp.stack(results)
    summed = lax.psum_scatter(
        chi_parts.astype(jnp.bfloat16), "band", scatter_dimension=0, tiled=True
    ).astype(jnp.float32)
    return -summed


def solution(mesh):
    return jax.shard_map(
        per_device,
        mesh=mesh,
        in_specs=(
            P(),
            P(("band", "grow", "gcol"), None),
            P(),
            P(),
            P(),
            P(None, ("band", "grow", "gcol")),
            P(("band", "grow", "gcol")),
        ),
        out_specs=P("band", "grow", "gcol"),
        check_vma=False,
    )
```

profile of v0, /device:TPU:0, one launch (start us, length us, event | category | flops | bytes accessed | tf_op | source)
XLA Modules:
  0.0 316.5 jit_solution(12738312803121980333)
XLA Ops:
  6.5 0.7 all-gather.5.cloned.1.call-update
  8.1 1.2 dynamic-slice
  9.4 0.8 dynamic-update-slice
  10.1 1.9 all-reduce
  12.1 0.6 fusion.92
  12.6 2.0 all-gather
  14.7 0.1 reshape.235
  14.8 0.6 fusion.75
  15.4 0.7 gather_fusion
  17.4 0.7 gather_fusion.2
  18.1 0.8 mul.116
  18.9 1.3 gather_fusion.5
  20.2 3.7 %gather_fusion.1 = bf16[10,98304]{1,0:T(8,128)(2,1)} fusion(bf16[16,98304]{1,0:T(8,128)(2,1)S(1)} %copy-done, s32[1024]{0:T(1024)S(1)} %pad_clamp_fusion.2), kind=kCustom, calls=%fused_computation.1 | custom fusion | bytes 3932200 | tf_op jit(solution)/shard_map/gather | solution.py:29
  23.9 0.7 fusion.73
  24.6 0.7 gather_fusion.4
  25.4 0.0 all-gather.5.cloned.1.call-done
  25.4 1.8 reshape.237
  27.2 3.6 %gather_fusion.3 = bf16[10,98304]{1,0:T(8,128)(2,1)} fusion(bf16[8,98304]{1,0:T(8,128)(2,1)S(1)} %reshape.237, s32[1024]{0:T(1024)S(1)} %pad_clamp_fusion.1), kind=kCustom, calls=%fused_computation.3 | custom fusion | bytes 3932200 | tf_op jit(solution)/shard_map/gather | solution.py:29
  30.9 6.1 %convert_multiply_fusion = f32[10,98304]{1,0:T(8,128)} fusion(bf16[10,98304]{1,0:T(8,128)(2,1)} %gather_fusion.3, bf16[10,98304]{1,0:T(8,128)(2,1)} %gather_fusion.1), kind=kLoop, calls=%fused_computation.12 | loop fusion | flops 2949120 | bytes 7864320 | tf_op jit(solution)/shard_map/mul | solution.py:29
  37.0 10.8 %mul.112 = f32[10,32,48,64]{3,2,1,0:T(8,128)} reshape(f32[10,98304]{1,0:T(8,128)} %convert_multiply_fusion) | data formatting | bytes 7864320 | tf_op jit(solution)/shard_map/mul | solution.py:29
  47.8 28.5 %fusion.12 = f32[10,32,48,32]{2,3,1,0:T(8,128)S(1)} fusion(f32[10,32,48,64]{3,2,1,0:T(8,128)} %mul.112, s32[32]{0:T(128)S(1)} %get-tuple-element.17, s32[32]{0:T(128)S(1)} %get-tuple-element.18, pred[32]{0:T(512)(128)(4,1)S(1)} %compare_and_fusion), kind=kOutput, calls=%fused_computation.29 | convolution fusion | flops 377522176 | bytes 5898528 | tf_op jit(solution)/shard_map/pabc,kc->pabk/dot_general | solution.py:33
  76.3 20.5 %convolution_bitcast_fusion = f32[10,32,24,32]{3,2,1,0:T(8,128)S(1)} fusion(f32[10,32,48,32]{2,3,1,0:T(8,128)S(1)} %fusion.12, s32[24]{0:T(128)S(1)} %get-tuple-element.19, s32[24]{0:T(128)S(1)} %get-tuple-element.20, pred[24]{0:T(512)(128)(4,1)S(1)} %compare_and_fusion.1), kind=kOutput, calls=%fused_computation.17 | convolution fusion | flops 141571584 | bytes 2949336 | tf_op jit(solution)/shard_map/pabc,kb->pakc/dot_general | solution.py:34
  96.8 2.8 fusion.4
  99.6 1.9 copy.18
  101.4 2.5 reshape.180
  103.9 0.1 multiply_convert_fusion.2
  104.0 0.9 copy.19
  104.9 5.0 %all-to-all-start.1 = ((bf16[10,4,3072]{2,0,1:T(8,128)(2,1)}), bf16[10,4,3072]{2,0,1:T(8,128)(2,1)S(1)}, u32[]{:S(2)}, u32[]{:S(2)}) async-start(bf16[10,4,3072]{2,0,1:T(8,128)(2,1)} %copy.19), calls=%async_computation.1 | async-start | bytes 786432 | tf_op jit(solution)/shard_map/all_to_all | solution.py:93
  109.9 0.1 multiply_bitcast_fusion
  110.0 41.6 %all-gather.2 = f32[16,10,2]{1,2,0:T(2,128)S(1)} all-gather(f32[1,10,2]{1,2,0:T(2,128)S(1)} %multiply_bitcast_fusion), channel_id=1, replica_groups=mesh['band'=2,'grow'=4,'gcol'=4] {'grow','gcol'}, dimensions={0}, use_global_device_ids=true | all-gather | bytes 1360 | tf_op jit(solution)/shard_map/all_gather | solution.py:101
  151.5 0.1 reshape.239
  151.6 0.1 mul.123
  151.7 0.1 mul.126
  151.8 3.5 %all-to-all-start = ((bf16[10,4,3072]{2,0,1:T(8,128)(2,1)}), bf16[10,4,3072]{2,0,1:T(8,128)(2,1)S(1)}, u32[]{:S(2)}, u32[]{:S(2)}) async-start(bf16[10,4,3072]{2,0,1:T(8,128)(2,1)} %copy.19), calls=%async_computation | async-start | bytes 786432 | tf_op jit(solution)/shard_map/all_to_all | solution.py:85
  155.3 0.0 reduce-scatter.2.cloned.1.call-start
  155.4 0.1 all_to_all.33
  155.5 24.0 %all_gather.22 = bf16[160,1,3072]{2,0,1:T(8,128)(2,1)} all-gather(bf16[40,1,3072]{2,0,1:T(8,128)(2,1)S(1)} %all_to_all.33), channel_id=1, replica_groups=mesh['band'=2,'grow'=4,'gcol'=4] {'grow'}, dimensions={0}, use_global_device_ids=true | all-gather | bytes 1228800 | tf_op jit(solution)/shard_map/all_gather | solution.py:100
  179.4 1.3 reshape.182
  180.8 2.4 multiply_convert_fusion.1
  183.2 0.1 all_to_all.29
  183.3 10.4 %all_gather.21 = bf16[160,1,3072]{2,0,1:T(8,128)(2,1)S(1)} all-gather(bf16[40,1,3072]{2,0,1:T(8,128)(2,1)S(1)} %all_to_all.29), channel_id=1, replica_groups=mesh['band'=2,'grow'=4,'gcol'=4] {'gcol'}, dimensions={0}, use_global_device_ids=true | all-gather | bytes 1228800 | tf_op jit(solution)/shard_map/all_gather | solution.py:92
  193.7 0.4 reshape.181
  194.1 10.7 %fusion = bf16[1,3072,3072]{2,1,0:T(8,128)(2,1)} fusion(bf16[4,4,10,3072]{3,2,1,0:T(8,128)(2,1)S(1)} %reshape.181, bf16[4,4,10,3072]{3,2,1,0:T(8,128)(2,1)} %get-tuple-element.7), kind=kOutput, calls=%fused_computation.10 | convolution fusion | flops 3029336064 | bytes 20840448 | tf_op jit(solution)/shard_map/crsi,rcsj->ij/dot_general | solution.py:108
  204.7 9.3 %fusion.1 = bf16[1,3072,3072]{2,1,0:T(8,128)(2,1)} fusion(bf16[4,4,10,3072]{3,2,1,0:T(8,128)(2,1)S(1)} %reshape.181, bf16[4,4,10,3072]{3,2,1,0:T(8,128)(2,1)S(1)} %copy-done.3), kind=kOutput, calls=%fused_computation.11 | convolution fusion | flops 3029336064 | bytes 20840448 | tf_op jit(solution)/shard_map/crsi,rcsj->ij/dot_general | solution.py:108
  214.1 25.9 %pad_maximum_fusion = bf16[2,3072,3072]{2,1,0:T(8,128)(2,1)} fusion(bf16[1,3072,3072]{2,1,0:T(8,128)(2,1)} %fusion.1, bf16[1,3072,3072]{2,1,0:T(8,128)(2,1)} %fusion), kind=kLoop, calls=%fused_computation.6 | loop fusion | flops 18874368 | bytes 75497472 | tf_op jit(solution)/shard_map/stack | solution.py:110
  240.0 0.0 reduce-scatter.2.cloned.1.call-update
  240.0 47.9 %reduce-scatter.2.cloned.1.call-done = bf16[1,3072,3072]{2,1,0:T(8,128)(2,1)} async-done(((bf16[2,3072,3072]{2,1,0:T(8,128)(2,1)}), bf16[1,3072,3072]{2,1,0:T(8,128)(2,1)}) %reduce-scatter.2.cloned.1.call-update) | async-done | bytes 18874384 | tf_op jit(solution)/shard_map/reduce_scatter | solution.py:111
  287.9 21.3 %convert_negate_fusion = f32[1,3072,3072]{2,1,0:T(8,128)} fusion(bf16[1,3072,3072]{2,1,0:T(8,128)(2,1)} %reduce-scatter.2.cloned.1.call-done), kind=kLoop, calls=%fused_computation.9 | loop fusion | flops 18874368 | bytes 56623104 | tf_op jit(solution)/shard_map/neg | solution.py:114
  (30 shorter events, 0.2 us)
Async XLA Ops:
  6.5 13.7 %copy-start = (bf16[16,98304]{1,0:T(8,128)(2,1)S(1)}, bf16[16,98304]{1,0:T(8,128)(2,1)}, u32[]{:S(2)}) copy-start(bf16[16,98304]{1,0:T(8,128)(2,1)} %param.7) | copy-start | bytes 9437188
  6.5 18.9 %all-gather.5.cloned.1.call-start = ((), (), s32[]{:S(2)}) async-start(), calls=%async_computation.4 | async-start | bytes 2359296 | tf_op jit(solution)/shard_map/all_gather | solution.py:64
  20.2 4.4 %copy-start.2 = (f32[128]{0:T(128)S(1)}, f32[128]{0:T(128)}, u32[]{:S(2)}) copy-start(f32[128]{0:T(128)} %param.10) | copy-start | bytes 1540
  104.9 47.0 %all-to-all-start.1 = ((bf16[10,4,3072]{2,0,1:T(8,128)(2,1)}), bf16[10,4,3072]{2,0,1:T(8,128)(2,1)S(1)}, u32[]{:S(2)}, u32[]{:S(2)}) async-start(bf16[10,4,3072]{2,0,1:T(8,128)(2,1)} %copy.19), calls=%async_computation.1 | async-start | bytes 786432 | tf_op jit(solution)/shard_map/all_to_all | solution.py:93
  151.8 31.4 %all-to-all-start = ((bf16[10,4,3072]{2,0,1:T(8,128)(2,1)}), bf16[10,4,3072]{2,0,1:T(8,128)(2,1)S(1)}, u32[]{:S(2)}, u32[]{:S(2)}) async-start(bf16[10,4,3072]{2,0,1:T(8,128)(2,1)} %copy.19), calls=%async_computation | async-start | bytes 786432 | tf_op jit(solution)/shard_map/all_to_all | solution.py:85
  155.3 132.6 %reduce-scatter.2.cloned.1.call-start = ((), (), s32[]{:S(2)}) async-start(), calls=%async_computation.3 | async-start | bytes 56623104 | tf_op jit(solution)/shard_map/reduce_scatter | solution.py:111
  194.0 10.7 %copy-start.3 = (bf16[4,4,10,3072]{3,2,1,0:T(8,128)(2,1)S(1)}, bf16[4,4,10,3072]{3,2,1,0:T(8,128)(2,1)}, u32[]{:S(2)}) copy-start(bf16[4,4,10,3072]{3,2,1,0:T(8,128)(2,1)} %get-tuple-element.8) | copy-start | bytes 2949124
  287.9 21.3 %copy-start.1 = (bf16[16,98304]{1,0:T(8,128)(2,1)S(1)}, bf16[16,98304]{1,0:T(8,128)(2,1)}, u32[]{:S(2)}) copy-start(bf16[16,98304]{1,0:T(8,128)(2,1)} %param.7) | copy-start | bytes 9437188
Sparse Core Ops, SparseCore 0:
  8.9 12.4 all-gather.4
  240.1 47.7 reduce-scatter.1
where the time goes:
time: 321 us; the launch traced here: 317 us
  blocking collectives  79.9 us (25%)
  matrix products  71.7 us (22%)
  other arithmetic  57.4 us (18%)
  waiting for transfers between devices  48.7 us (15%)
  local copies, waits for them, and re-layouts  34.1 us (11%)
  between operations  16.2 us (5%)
  starting transfers between devices  8.52 us (3%)
    reduce_scatter x1, waiting for transfers between devices, per_device(): lax.psum_scatter(chi_parts.astype(jnp.bfloat16), 'band', scatter_dimensio...  47.9 us
    all_gather x1, blocking collectives, per_device(): lax.all_gather(pair_weight, ('grow', 'gcol'), axis=1, tiled=True)  41.6 us
    dot_general x1, matrix products, densities(): jnp.einsum('pabc,kc->pabk', lattice, pruned_table(N3, M3), precision=high...  28.5 us
    another operation x1, other arithmetic, per_device(): chi_parts = jnp.stack(results)  25.9 us
    all_gather x1, blocking collectives, per_device(): col_panel = lax.all_gather(col_panel, 'grow', axis=0, tiled=True)  24 us
    neg x1, other arithmetic, per_device(): return -summed  21.3 us
    dot_general x1, matrix products, densities(): jnp.einsum('pabc,kb->pakc', lattice, pruned_table(N2, M2), precision=high...  20.5 us
    dot_general x2, matrix products, per_device(): jnp.einsum('crsi,rcsj->ij', row_four, weighted, preferred_element_type=jn...  20 us
  transfers between devices with their start and end apart: 4, of which 1 were waited for; matrix products, arithmetic and copies ran while one was open for 5% of the time, Pallas kernels for 0%

commit v1 on v0

v1 whole, which is shorter than its diff:
```python
import functools
import math

import jax
import jax.numpy as jnp
import ml_dtypes
import numpy as np
from jax import lax
from jax.experimental import pallas as pl
from jax.experimental.pallas import tpu as pltpu
from jax.sharding import PartitionSpec as P

N1 = 16
N2 = 24
N3 = 32
M1 = 32
M2 = 48
M3 = 64
SLOTS = 20
FREQS = 2
LANES = 128
MESH = pl.DeviceIdType.MESH


def pruned_table(keep, length):
    wave = (np.arange(keep)[:, None] - keep // 2) % length
    angles = (wave * np.arange(length)[None, :] % length) * (2.0 * math.pi / length)
    return (np.cos(angles) + np.sin(angles)) / math.sqrt(length)


def density_kernel(count, val_ref, con_ref, v_ref, c_ref, first_ref, rest_ref, root_ref, out_ref, prod, mid):
    slot = pl.program_id(0)
    rows = pl.ds(pl.multiple_of(slot * M1, M1), M1)
    prod[rows, :] = (v_ref[0].astype(jnp.float32) * c_ref[0].astype(jnp.float32)).astype(jnp.bfloat16)

    @pl.when(slot == count - 1)
    def _():
        plane = M2 * M3
        step = 512
        for at in range(0, plane, step):
            mid[:, at : at + step] = jnp.dot(
                first_ref[...], prod[:, at : at + step], preferred_element_type=jnp.float32
            ).astype(jnp.bfloat16)
        kept = N2 * N3
        step = 256
        for at in range(0, kept, step):
            full = jnp.dot(mid[...], rest_ref[:, at : at + step], preferred_element_type=jnp.float32)
            full = full.reshape(count, N1, step) * root_ref[:, at : at + step][None]
            out_ref[:, :, at : at + step] = full.astype(jnp.bfloat16)


def densities(valence, conduction, coulomb_root, val_index, con_index):
    count = val_index.shape[0]
    plane = M2 * M3
    kept = N2 * N3
    first = np.kron(np.eye(count), pruned_table(N1, M1)).astype(ml_dtypes.bfloat16)
    rest = np.kron(pruned_table(N2, M2), pruned_table(N3, M3)).T.astype(ml_dtypes.bfloat16)
    whole = lambda shape: pl.BlockSpec(shape, lambda p, v, c: (0,) * len(shape))
    return pl.pallas_call(
        functools.partial(density_kernel, count),
        out_shape=jax.ShapeDtypeStruct((count, N1, kept), jnp.bfloat16),
        grid_spec=pltpu.PrefetchScalarGridSpec(
            num_scalar_prefetch=2,
            grid=(count,),
            in_specs=[
                pl.BlockSpec((1, M1, plane), lambda p, v, c: (v[p], 0, 0)),
                pl.BlockSpec((1, M1, plane), lambda p, v, c: (c[p], 0, 0)),
                whole((count * N1, count * M1)),
                whole((plane, kept)),
                whole((N1, kept)),
            ],
            out_specs=whole((count, N1, kept)),
            scratch_shapes=[
                pltpu.VMEM((count * M1, plane), jnp.bfloat16),
                pltpu.VMEM((count * N1, plane), jnp.bfloat16),
            ],
        ),
        compiler_params=pltpu.CompilerParams(vmem_limit_bytes=40 * 2**20),
        name="pair_density",
    )(
        val_index,
        con_index,
        valence,
        conduction,
        jnp.asarray(first),
        jnp.asarray(rest),
        coulomb_root.reshape(N1, kept),
    )


def exchange_kernel(
    grow, gcol, rows_in, cols_in, rows, cols,
    local_sem, r1s, r1r, c1s, c1r, r2s, r2r, c2s, c2r, r3s, r3r, c3s, c3r,
):
    b = lax.axis_index("band")
    g = lax.axis_index("grow")
    c = lax.axis_index("gcol")
    sibling = (1 - b, g, c)
    near_g = [(g + i) % grow for i in range(grow)]
    near_c = [(c + i) % gcol for i in range(gcol)]
    back_g = [(g + grow - i) % grow for i in range(grow)]
    back_c = [(c + gcol - i) % gcol for i in range(gcol)]

    barrier = pltpu.get_barrier_semaphore()
    pl.semaphore_signal(barrier, inc=1, device_id=sibling, device_id_type=MESH)
    for i in range(1, grow):
        pl.semaphore_signal(barrier, inc=1, device_id=(b, near_g[i], c), device_id_type=MESH)
    for i in range(1, gcol):
        pl.semaphore_signal(barrier, inc=1, device_id=(b, g, near_c[i]), device_id_type=MESH)
    own_row = pltpu.make_async_copy(rows_in.at[g], rows.at[b, c, g], local_sem.at[0])
    own_col = pltpu.make_async_copy(cols_in.at[c], cols.at[b, c, g], local_sem.at[1])
    own_row.start()
    own_col.start()
    pl.semaphore_wait(barrier, grow + gcol - 1)

    sent = []

    def send(src, dst, send_sem, recv_sem, target):
        copy = pltpu.make_async_remote_copy(
            src_ref=src, dst_ref=dst, send_sem=send_sem, recv_sem=recv_sem,
            device_id=target, device_id_type=MESH,
        )
        copy.start()
        sent.append(copy)

    def arrive(ref, send_sem, recv_sem):
        pltpu.make_async_remote_copy(
            src_ref=ref, dst_ref=ref, send_sem=send_sem, recv_sem=recv_sem,
            device_id=sibling, device_id_type=MESH,
        ).wait_recv()

    for i in range(1, gcol):
        send(cols_in.at[near_c[i]], cols.at[b, c, g], c1s.at[i], c1r.at[i], (b, g, near_c[i]))
    for i in range(1, grow):
        send(rows_in.at[near_g[i]], rows.at[b, c, g], r1s.at[i], r1r.at[i], (b, near_g[i], c))

    own_col.wait()
    for i in range(1, gcol):
        arrive(cols.at[b, back_c[i], g], c1s.at[i], c1r.at[i])
    block = cols.at[b, :, g]
    for i in range(1, grow):
        send(block, block, c2s.at[i], c2r.at[i], (b, near_g[i], c))
    send(block, block, c3s.at[0], c3r.at[0], sibling)

    own_row.wait()
    for i in range(1, grow):
        arrive(rows.at[b, c, back_g[i]], r1s.at[i], r1r.at[i])
    block = rows.at[b, c]
    for i in range(1, gcol):
        send(block, block, r2s.at[i], r2r.at[i], (b, g, near_c[i]))
    send(block, block, r3s.at[0], r3r.at[0], sibling)

    for i in range(1, gcol):
        block = rows.at[b, back_c[i]]
        arrive(block, r2s.at[i], r2r.at[i])
        send(block, block, r3s.at[i], r3r.at[i], sibling)
    for i in range(1, grow):
        block = cols.at[b, :, back_g[i]]
        arrive(block, c2s.at[i], c2r.at[i])
        send(block, block, c3s.at[i], c3r.at[i], sibling)
    for i in range(gcol):
        arrive(rows.at[1 - b, back_c[i]], r3s.at[i], r3r.at[i])
    for i in range(grow):
        arrive(cols.at[1 - b, :, back_g[i]], c3s.at[i], c3r.at[i])
    for copy in sent:
        copy.wait_send()


def exchange(rows_in, cols_in, grow, gcol):
    sem = lambda n: pltpu.SemaphoreType.DMA((n,))
    return pl.pallas_call(
        functools.partial(exchange_kernel, grow, gcol),
        out_shape=(
            jax.ShapeDtypeStruct((2, gcol, grow) + rows_in.shape[1:], rows_in.dtype),
            jax.ShapeDtypeStruct((2, gcol, grow) + cols_in.shape[1:], cols_in.dtype),
        ),
        in_specs=[pl.BlockSpec(memory_space=pl.ANY)] * 2,
        out_specs=(pl.BlockSpec(memory_space=pl.ANY),) * 2,
        scratch_shapes=[sem(2)]
        + [sem(grow)] * 2 + [sem(gcol)] * 2
        + [sem(gcol)] * 2 + [sem(grow)] * 2
        + [sem(gcol)] * 2 + [sem(grow)] * 2,
        compiler_params=pltpu.CompilerParams(collective_id=0, has_side_effects=True),
        name="panel_exchange",
    )(rows_in, cols_in)


def per_device(
    valence_orbitals,
    conduction_orbitals,
    valence_energy,
    conduction_energy,
    coulomb_root,
    pair_bands,
    slot_counts,
):
    grow_size = lax.axis_size("grow")
    gcol_size = lax.axis_size("gcol")
    chips = grow_size * gcol_size
    factor = 1.0 / math.sqrt(2 * chips * SLOTS)
    local_slots = pair_bands.shape[1]
    held_con = conduction_orbitals.shape[0]
    half_slots = local_slots // 2
    band_rank = lax.axis_index("band")

    valence = valence_orbitals.reshape(-1, M1, M2 * M3)
    both_con = lax.all_gather(
        conduction_orbitals.reshape(held_con, M1, M2 * M3), "band", axis=0, tiled=True
    )
    facts = jnp.concatenate([pair_bands.reshape(-1), slot_counts])
    facts = lax.all_gather(facts, ("band", "grow", "gcol"), axis=0, tiled=False)
    facts = facts.reshape(2, chips, -1)
    lists = facts[:, :, : 2 * local_slots].reshape(2, chips, 2, local_slots)
    counts = facts[:, :, 2 * local_slots]
    position = jnp.arange(local_slots)[None, :]
    first_count = counts[0][:, None]
    source = jnp.where(position < first_count, position, local_slots + position - first_count)
    source = jnp.minimum(source, 2 * local_slots - 1)
    is_live = position < first_count + counts[1][:, None]
    chip_lists = lists.transpose(2, 1, 0, 3).reshape(2, chips, 2 * local_slots)
    val_all = jnp.take_along_axis(chip_lists[0], source, axis=1)
    con_all = jnp.take_along_axis(chip_lists[1], source, axis=1)
    local_all = con_all % held_con + source // local_slots * held_con

    my_chip = lax.axis_index("grow") * gcol_size + lax.axis_index("gcol")
    mine = lambda x: lax.dynamic_slice(x, (my_chip, band_rank * half_slots), (1, half_slots))[0]
    density = densities(valence, both_con, coulomb_root, mine(val_all), mine(local_all))

    row_block = N1 * N2 * N3 // grow_size
    col_block = N1 * N2 * N3 // gcol_size

    def wire(blocks, block):
        parts = density.reshape(half_slots, blocks, block // LANES, LANES).transpose(1, 0, 2, 3)
        return parts.reshape(blocks, half_slots * (block // LANES), LANES)

    row_panel, col_panel = exchange(
        wire(grow_size, row_block), wire(gcol_size, col_block), grow_size, gcol_size
    )
    row_panel = row_panel.reshape(2 * chips * half_slots, row_block)
    col_panel = col_panel.reshape(2 * chips * half_slots, col_block)

    gap = conduction_energy[con_all] - valence_energy[val_all]
    frequency = band_rank.astype(jnp.float32)
    weight = jnp.where(is_live, 2.0 * gap / (gap * gap + frequency * frequency), 0.0) * factor
    weight = weight.reshape(grow_size, gcol_size, 2, half_slots).transpose(2, 1, 0, 3).reshape(-1, 1)
    weighted = (col_panel.astype(jnp.float32) * -weight).astype(jnp.bfloat16)
    chi = lax.dot_general(
        row_panel, weighted, (((0,), (0,)), ((), ())), preferred_element_type=jnp.float32
    )
    return chi[None]


def solution(mesh):
    return jax.shard_map(
        per_device,
        mesh=mesh,
        in_specs=(
            P(),
            P(("band", "grow", "gcol"), None),
            P(),
            P(),
            P(),
            P(None, ("band", "grow", "gcol")),
            P(("band", "grow", "gcol")),
        ),
        out_specs=P("band", "grow", "gcol"),
        check_vma=False,
    )
```

time: 321 us -> 145 us (0.45)
  the two profiles are of different devices: /device:TPU:0 before, /device:TPU:11 now
where the time goes in v1:
time: 145 us
  blocking collectives  39.5 us (27%)
  Pallas kernels  38.5 us (27%)
  local copies, waits for them, and re-layouts  30 us (21%)
  matrix products  18.1 us (12%)
  between operations  14.3 us (10%)
  other arithmetic  4.12 us (3%)
    unnamed x1, blocking collectives  39.5 us
    pallas_call x1, Pallas kernels, exchange(): pl.pallas_call(functools.partial(exchange_kernel, grow, gcol), out_shape=...  35.8 us
    dot_general x1, matrix products, per_device(): lax.dot_general(row_panel, weighted, (((0,), (0,)), ((), ())), preferred_...  18.1 us
    unnamed x17, local copies, waits for them, and re-layouts  11.2 us
    gather x2, local copies, waits for them, and re-layouts, per_device(): gap = conduction_energy[con_all] - valence_energy[val_all]  4.71 us
    convert_element_type x1, local copies, waits for them, and re-layouts, per_device(): weighted = (col_panel.astype(jnp.float32) * -weight).astype(jnp.bfloat16)  4 us
    convert_element_type x1, other arithmetic, per_device(): weighted = (col_panel.astype(jnp.float32) * -weight).astype(jnp.bfloat16)  3.32 us
  transfers between devices with their start and end apart: 1, of which 0 were waited for; matrix products, arithmetic and copies ran while one was open for 11% of the time, Pallas kernels for 0%

profile of v1, /device:TPU:11, one launch (start us, length us, event | category | flops | bytes accessed | tf_op | source)
XLA Modules:
  0.0 144.6 jit_solution(142307259866501416)
XLA Ops:
  6.5 0.0 copy-start
  6.5 0.0 all-gather.3.cloned.1.call-start
  6.5 2.3 %copy.29 = bf16[1,4,32,3072]{3,2,1,0:T(8,128)(2,1)} copy(bf16[1,4,32,3072]{3,1,2,0:T(4,128)(2,1)} %bitcast.35) | data formatting | bytes 1572864
  8.8 0.0 all-gather.3.cloned.1.call-update
  9.5 0.0 copy-done.6
  9.5 0.1 reshape.101
  9.6 0.2 add_dynamic-update-slice_fusion
  9.8 39.5 %all-reduce = s32[1312]{0:T(1024)S(1)} all-reduce(s32[1312]{0:T(1024)S(1)} %add_dynamic-update-slice_fusion), channel_id=2, replica_groups=mesh['band'=2,'grow'=4,'gcol'=4] {'band','grow','gcol'}, use_global_device_ids=true, to_apply=%add | all-reduce | flops 1312 | bytes 10496
  49.3 0.1 reshape.102
  49.4 0.2 fusion.4
  49.6 0.1 add.77
  49.7 0.1 bitcast_or_fusion
  49.8 0.1 reshape.166
  49.9 0.1 reshape.103
  50.0 0.1 squeeze.15
  50.1 2.5 %gather_fusion.3 = s32[320]{0:T(512)S(1)} fusion(s32[16,40]{1,0:T(8,128)S(1)} %squeeze.15, s32[320]{0:T(512)S(1)} %reshape.166), kind=kCustom, calls=%fused_computation.1.clone | custom fusion | bytes 5120 | tf_op jit(solution)/shard_map/jit(take_along_axis)/gather | solution.py:222
  52.6 0.1 reshape.174
  52.7 0.1 squeeze.13
  52.8 2.5 %gather_fusion.2 = s32[320]{0:T(512)S(1)} fusion(s32[16,40]{1,0:T(8,128)S(1)} %squeeze.13, s32[320]{0:T(512)S(1)} %reshape.166), kind=kCustom, calls=%fused_computation.clone | custom fusion | bytes 5120 | tf_op jit(solution)/shard_map/jit(take_along_axis)/gather | solution.py:221
  55.3 0.1 reshape.169
  55.4 0.1 add_select_fusion
  55.5 0.1 reshape.125
  55.6 0.1 reshape.133
  55.7 2.4 %gather_fusion = f32[320]{0:T(512)S(1)} fusion(f32[128]{0:T(128)S(1)} %copy-done, s32[1024]{0:T(1024)S(1)} %pad_clamp_fusion.1), kind=kCustom, calls=%fused_computation.2 | custom fusion | bytes 3840 | tf_op jit(solution)/shard_map/gather | solution.py:242
  58.1 0.0 copy-start.4
  58.1 0.6 copy-done.4
  58.7 2.3 %gather_fusion.1 = f32[320]{0:T(512)S(1)} fusion(f32[16]{0:T(128)S(1)} %copy-done.4, s32[1024]{0:T(1024)S(1)} %pad_clamp_fusion), kind=kCustom, calls=%fused_computation.3 | custom fusion | bytes 3840 | tf_op jit(solution)/shard_map/gather | solution.py:242
  61.1 0.1 div.15
  61.2 0.1 fusion.2
  61.3 0.0 copy-done.5
  61.4 0.1 mul.56
  61.5 0.1 mul.57
  61.6 3.6 %copy.26 = bf16[2,8,32,3072]{3,2,1,0:T(8,128)(2,1)S(1)} copy(bf16[2,8,32,3072]{3,1,2,0:T(8,128)(2,1)} %bitcast.31) | data formatting | bytes 6291456
  65.2 0.1 select_compare_fusion
  65.3 0.1 dynamic-slice_bitcast_fusion
  65.4 0.0 all-gather.3.cloned.1.call-done.c_ref
  65.5 0.0 copy-start.1
  65.5 2.3 %copy-done.1 = bf16[3072,768]{1,0:T(8,128)(2,1)S(1)} copy-done((bf16[3072,768]{1,0:T(8,128)(2,1)S(1)}, bf16[3072,768]{1,0:T(8,128)(2,1)}, u32[]{:S(2)}) %copy-start.1) | copy-done | bytes 4718616
  67.8 1.4 copy-done.2
  69.2 0.9 copy-done.3
  70.1 2.7 %pair_density.1 = bf16[10,16,768]{2,1,0:T(8,128)(2,1)S(1)} custom-call(s32[10]{0:T(128)S(1)} %get-tuple-element.21.val_ref, s32[10]{0:T(128)S(1)} %get-tuple-element.22.con_ref, bf16[16,32,3072]{2,1,0:T(8,128)(2,1)S(1)} %bitcast.30, bf16[8,32,3072]{2,1,0:T(8,128)(2,1)S(1)} %copy-done.2, bf16[160,320]{1,0:T(8,128)(2,1)S(1)} %copy-done.3, ...), custom_call_target="tpu_custom_call" | custom-call | tf_op jit(solution)/shard_map/pair_density/pallas_call | solution.py:59
  72.8 0.2 reshape.107
  73.0 0.7 copy.24
  73.7 35.8 %panel_exchange.1 = (bf16[2,4,4,240,128]{4,3,2,1,0:T(8,128)(2,1)}, bf16[2,4,4,240,128]{4,3,2,1,0:T(8,128)(2,1)}) custom-call(bf16[4,240,128]{2,1,0:T(8,128)(2,1)} %bitcast.33, bf16[4,240,128]{2,1,0:T(8,128)(2,1)} %bitcast.34), custom_call_target="tpu_custom_call" | custom-call | tf_op jit(solution)/shard_map/panel_exchange/pallas_call | solution.py:171
  109.6 2.8 %reshape.109 = bf16[320,3072]{1,0:T(8,128)(2,1)S(1)} reshape(bf16[2,4,4,240,128]{4,3,2,1,0:T(8,128)(2,1)} %get-tuple-element.8) | data formatting | bytes 3932160 | tf_op jit(solution)/shard_map/reshape | solution.py:239
  112.3 3.3 %multiply_convert_fusion = bf16[2,4,4,240,128]{4,3,2,1,0:T(8,128)(2,1)} fusion(bf16[2,4,4,240,128]{4,3,2,1,0:T(8,128)(2,1)} %get-tuple-element.9, f32[2,4,4,240]{3,2,1,0:T(4,128)S(1)} %mul.57), kind=kLoop, calls=%fused_computation.5 | loop fusion | flops 2949120 | bytes 3962880 | tf_op jit(solution)/shard_map/convert_element_type | solution.py:246
  115.7 4.0 %convert_element_type.16 = bf16[320,3072]{1,0:T(8,128)(2,1)} reshape(bf16[2,4,4,240,128]{4,3,2,1,0:T(8,128)(2,1)} %multiply_convert_fusion) | data formatting | bytes 3932160 | tf_op jit(solution)/shard_map/convert_element_type | solution.py:246
  119.7 18.1 %convolution_bitcast_fusion = f32[1,3072,3072]{2,1,0:T(8,128)} fusion(bf16[320,3072]{1,0:T(8,128)(2,1)S(1)} %reshape.109, bf16[320,3072]{1,0:T(8,128)(2,1)} %convert_element_type.16), kind=kOutput, calls=%fused_computation.4 | convolution fusion | flops 6039797760 | bytes 41680896 | tf_op jit(solution)/shard_map/dot_general | solution.py:247
  (16 shorter events, 0.1 us)
Async XLA Ops:
  6.5 49.2 %copy-start = (f32[128]{0:T(128)S(1)}, f32[128]{0:T(128)}, u32[]{:S(2)}) copy-start(f32[128]{0:T(128)} %param.14) | copy-start | bytes 1540
  6.5 3.0 %copy-start.6 = (s32[2,20]{1,0:T(2,128)S(1)}, s32[2,20]{1,0:T(2,128)}, u32[]{:S(2)}) copy-start(s32[2,20]{1,0:T(2,128)} %param.16) | copy-start | bytes 484
  6.5 58.9 %all-gather.3.cloned.1.call-start = ((), (), s32[]{:S(2)}) async-start(), calls=%async_computation | async-start | bytes 2359296 | tf_op jit(solution)/shard_map/all_gather | solution.py:207
  58.1 0.7 copy-start.4
  58.7 2.6 %copy-start.5 = (f32[12288]{0:T(1024)S(1)}, f32[12288]{0:T(1024)}, u32[]{:S(2)}) copy-start(f32[12288]{0:T(1024)} %param.15) | copy-start | bytes 147460
  65.5 2.3 %copy-start.1 = (bf16[3072,768]{1,0:T(8,128)(2,1)S(1)}, bf16[3072,768]{1,0:T(8,128)(2,1)}, u32[]{:S(2)}) copy-start(bf16[3072,768]{1,0:T(8,128)(2,1)} %constant.73.clone.rest_ref) | copy-start | bytes 14155780
  67.8 1.4 copy-start.2
  69.2 0.9 copy-start.3
Sparse Core Ops, SparseCore 0:
  9.0 11.7 all-gather.2

commit v2 on v1

v2 whole, which is shorter than its diff:
```python
import functools
import math

import jax
import jax.numpy as jnp
import ml_dtypes
import numpy as np
from jax import lax
from jax.experimental import pallas as pl
from jax.experimental.pallas import tpu as pltpu
from jax.sharding import PartitionSpec as P

N1 = 16
N2 = 24
N3 = 32
M1 = 32
M2 = 48
M3 = 64
SLOTS = 20
FREQS = 2
LANES = 128
WEIGHT_ROWS = 16
MESH = pl.DeviceIdType.MESH


def pruned_table(keep, length):
    wave = (np.arange(keep)[:, None] - keep // 2) % length
    angles = (wave * np.arange(length)[None, :] % length) * (2.0 * math.pi / length)
    return (np.cos(angles) + np.sin(angles)) / math.sqrt(length)


def pick_slot(p, own, other, band, held_con):
    slots = (own.shape[0] - 1) // 2
    b = band[0]
    is_first = b == 0
    first = jnp.where(is_first, own[2 * slots], other[2 * slots])
    total = own[2 * slots] + other[2 * slots]
    position = b * (slots // 2) + p
    in_first = position < first
    column = jnp.where(in_first, position, jnp.minimum(position - first, slots - 1))
    is_own = in_first == is_first
    val = jnp.where(is_own, own[column], other[column])
    con = jnp.where(is_own, own[slots + column], other[slots + column])
    return val, con, con % held_con, is_own, position < total


def density_kernel(
    count, held_con, factor, own, other, band, val_energy, con_energy,
    v_ref, own_ref, other_ref, first_ref, rest_ref, root_ref, out_ref, weight_ref, prod, mid,
):
    slot = pl.program_id(0)
    val, con, _, is_own, live = pick_slot(slot, own, other, band, held_con)

    @pl.when(slot == 0)
    def _():
        weight_ref[...] = jnp.zeros_like(weight_ref)

    gap = jnp.full((1, LANES), con_energy[con] - val_energy[val], jnp.float32)
    keep = jnp.where(live, -factor, 0.0)
    for f in range(FREQS):
        response = 2.0 * gap / (gap * gap + float(f * f))
        weight_ref[f, pl.ds(slot, 1), :] = response * keep

    rows = pl.ds(pl.multiple_of(slot * M1, M1), M1)

    @pl.when(is_own)
    def _():
        prod[rows, :] = (v_ref[0].astype(jnp.float32) * own_ref[0].astype(jnp.float32)).astype(jnp.bfloat16)

    @pl.when(jnp.logical_not(is_own))
    def _():
        prod[rows, :] = (v_ref[0].astype(jnp.float32) * other_ref[0].astype(jnp.float32)).astype(jnp.bfloat16)

    @pl.when(slot == count - 1)
    def _():
        plane = M2 * M3
        step = 512
        for at in range(0, plane, step):
            mid[:, at : at + step] = jnp.dot(
                first_ref[...], prod[:, at : at + step], preferred_element_type=jnp.float32
            ).astype(jnp.bfloat16)
        kept = N2 * N3
        step = 256
        for at in range(0, kept, step):
            full = jnp.dot(mid[...], rest_ref[:, at : at + step], preferred_element_type=jnp.float32)
            full = full.reshape(count, N1, step) * root_ref[:, at : at + step][None]
            out_ref[:, :, at : at + step] = full.astype(jnp.bfloat16)


def densities(valence, con_own, con_other, coulomb_root, own, other, band, val_energy, con_energy, factor):
    count = (own.shape[0] - 1) // 4
    held_con = con_own.shape[0]
    plane = M2 * M3
    kept = N2 * N3
    first = np.kron(np.eye(count), pruned_table(N1, M1)).astype(ml_dtypes.bfloat16)
    rest = np.kron(pruned_table(N2, M2), pruned_table(N3, M3)).T.astype(ml_dtypes.bfloat16)
    whole = lambda shape: pl.BlockSpec(shape, lambda p, *_: (0,) * len(shape))
    choose = lambda at: lambda p, o, t, b, ve, ce: (pick_slot(p, o, t, b, held_con)[at], 0, 0)
    return pl.pallas_call(
        functools.partial(density_kernel, count, held_con, factor),
        out_shape=(
            jax.ShapeDtypeStruct((count, N1, kept), jnp.bfloat16),
            jax.ShapeDtypeStruct((FREQS, WEIGHT_ROWS, LANES), jnp.float32),
        ),
        grid_spec=pltpu.PrefetchScalarGridSpec(
            num_scalar_prefetch=5,
            grid=(count,),
            in_specs=[
                pl.BlockSpec((1, M1, plane), choose(0)),
                pl.BlockSpec((1, M1, plane), choose(2)),
                pl.BlockSpec((1, M1, plane), choose(2)),
                whole((count * N1, count * M1)),
                whole((plane, kept)),
                whole((N1, kept)),
            ],
            out_specs=(whole((count, N1, kept)), whole((FREQS, WEIGHT_ROWS, LANES))),
            scratch_shapes=[
                pltpu.VMEM((count * M1, plane), jnp.bfloat16),
                pltpu.VMEM((count * N1, plane), jnp.bfloat16),
            ],
        ),
        compiler_params=pltpu.CompilerParams(vmem_limit_bytes=40 * 2**20),
        name="pair_density",
    )(
        own, other, band, val_energy, con_energy,
        valence, con_own, con_other,
        jnp.asarray(first), jnp.asarray(rest), coulomb_root.reshape(N1, kept),
    )


def exchange_kernel(
    grow, gcol, rows_in, cols_in, weights_in, rows, cols, weights,
    local_sem, r1s, r1r, c1s, c1r, r2s, r2r, c2s, c2r, r3s, r3r, c3s, c3r, w1s, w1r, w2s, w2r, w3s, w3r,
):
    b = lax.axis_index("band")
    g = lax.axis_index("grow")
    c = lax.axis_index("gcol")
    sibling = (1 - b, g, c)
    near_g = [(g + i) % grow for i in range(grow)]
    near_c = [(c + i) % gcol for i in range(gcol)]
    back_g = [(g + grow - i) % grow for i in range(grow)]
    back_c = [(c + gcol - i) % gcol for i in range(gcol)]

    barrier = pltpu.get_barrier_semaphore()
    pl.semaphore_signal(barrier, inc=1, device_id=sibling, device_id_type=MESH)
    for i in range(1, grow):
        pl.semaphore_signal(barrier, inc=1, device_id=(b, near_g[i], c), device_id_type=MESH)
    for i in range(1, gcol):
        pl.semaphore_signal(barrier, inc=1, device_id=(b, g, near_c[i]), device_id_type=MESH)
    own_row = pltpu.make_async_copy(rows_in.at[g], rows.at[b, c, g], local_sem.at[0])
    own_col = pltpu.make_async_copy(cols_in.at[c], cols.at[b, c, g], local_sem.at[1])
    own_weight = pltpu.make_async_copy(weights_in, weights.at[b, c, g], local_sem.at[2])
    own_row.start()
    own_col.start()
    own_weight.start()
    pl.semaphore_wait(barrier, grow + gcol - 1)

    sent = []

    def send(src, dst, send_sem, recv_sem, target):
        copy = pltpu.make_async_remote_copy(
            src_ref=src, dst_ref=dst, send_sem=send_sem, recv_sem=recv_sem,
            device_id=target, device_id_type=MESH,
        )
        copy.start()
        sent.append(copy)

    def arrive(ref, send_sem, recv_sem):
        pltpu.make_async_remote_copy(
            src_ref=ref, dst_ref=ref, send_sem=send_sem, recv_sem=recv_sem,
            device_id=sibling, device_id_type=MESH,
        ).wait_recv()

    for i in range(1, gcol):
        send(weights_in, weights.at[b, c, g], w1s.at[i], w1r.at[i], (b, g, near_c[i]))
        send(cols_in.at[near_c[i]], cols.at[b, c, g], c1s.at[i], c1r.at[i], (b, g, near_c[i]))
    for i in range(1, grow):
        send(rows_in.at[near_g[i]], rows.at[b, c, g], r1s.at[i], r1r.at[i], (b, near_g[i], c))

    own_col.wait()
    own_weight.wait()
    for i in range(1, gcol):
        arrive(weights.at[b, back_c[i], g], w1s.at[i], w1r.at[i])
    block = weights.at[b, :, g]
    for i in range(1, grow):
        send(block, block, w2s.at[i], w2r.at[i], (b, near_g[i], c))
    send(block, block, w3s.at[0], w3r.at[0], sibling)
    for i in range(1, gcol):
        arrive(cols.at[b, back_c[i], g], c1s.at[i], c1r.at[i])
    block = cols.at[b, :, g]
    for i in range(1, grow):
        send(block, block, c2s.at[i], c2r.at[i], (b, near_g[i], c))
    send(block, block, c3s.at[0], c3r.at[0], sibling)

    own_row.wait()
    for i in range(1, grow):
        arrive(rows.at[b, c, back_g[i]], r1s.at[i], r1r.at[i])
    block = rows.at[b, c]
    for i in range(1, gcol):
        send(block, block, r2s.at[i], r2r.at[i], (b, g, near_c[i]))
    send(block, block, r3s.at[0], r3r.at[0], sibling)

    for i in range(1, gcol):
        block = rows.at[b, back_c[i]]
        arrive(block, r2s.at[i], r2r.at[i])
        send(block, block, r3s.at[i], r3r.at[i], sibling)
    for i in range(1, grow):
        block = weights.at[b, :, back_g[i]]
        arrive(block, w2s.at[i], w2r.at[i])
        send(block, block, w3s.at[i], w3r.at[i], sibling)
    for i in range(1, grow):
        block = cols.at[b, :, back_g[i]]
        arrive(block, c2s.at[i], c2r.at[i])
        send(block, block, c3s.at[i], c3r.at[i], sibling)
    for i in range(gcol):
        arrive(rows.at[1 - b, back_c[i]], r3s.at[i], r3r.at[i])
    for i in range(grow):
        arrive(weights.at[1 - b, :, back_g[i]], w3s.at[i], w3r.at[i])
        arrive(cols.at[1 - b, :, back_g[i]], c3s.at[i], c3r.at[i])
    for copy in sent:
        copy.wait_send()


def exchange(rows_in, cols_in, weights_in, grow, gcol):
    sem = lambda n: pltpu.SemaphoreType.DMA((n,))
    return pl.pallas_call(
        functools.partial(exchange_kernel, grow, gcol),
        out_shape=(
            jax.ShapeDtypeStruct((2, gcol, grow) + rows_in.shape[1:], rows_in.dtype),
            jax.ShapeDtypeStruct((2, gcol, grow) + cols_in.shape[1:], cols_in.dtype),
            jax.ShapeDtypeStruct((2, gcol, grow) + weights_in.shape, weights_in.dtype),
        ),
        in_specs=[pl.BlockSpec(memory_space=pl.ANY)] * 3,
        out_specs=(pl.BlockSpec(memory_space=pl.ANY),) * 3,
        scratch_shapes=[sem(3)]
        + [sem(grow)] * 2 + [sem(gcol)] * 2
        + [sem(gcol)] * 2 + [sem(grow)] * 2
        + [sem(gcol)] * 2 + [sem(grow)] * 2
        + [sem(gcol)] * 2 + [sem(grow)] * 2 + [sem(grow)] * 2,
        compiler_params=pltpu.CompilerParams(collective_id=0, has_side_effects=True),
        name="panel_exchange",
    )(rows_in, cols_in, weights_in)


def chi_kernel(count, tile, row_ref, col_ref, weight_ref, out_ref, lift, left, right):
    at_tile = pl.program_id(0)
    band = lax.axis_index("band")

    def unpack(panel, into, weighted):
        sources = into.shape[0] // count
        groups = into.shape[1] // LANES
        stride = count * groups
        total = sources * stride
        chunk = math.gcd(total, 512)

        def widen(s, carry):
            part = pl.ds(pl.multiple_of(s * chunk, chunk), chunk)
            lift[part, :] = panel[part, :].astype(jnp.float32)
            return carry

        lax.fori_loop(0, total // chunk, widen, 0)

        def place(p, carry):
            to = pl.ds(pl.multiple_of(p * sources, sources), sources)
            if weighted:
                scale = weight_ref[pl.ds(band * WEIGHT_ROWS + p, sources, stride=FREQS * WEIGHT_ROWS), :]
            for j in range(groups):
                piece = lift[pl.ds(p * groups + j, sources, stride=stride), :]
                if weighted:
                    piece = piece * scale
                into[to, j * LANES : (j + 1) * LANES] = piece.astype(jnp.bfloat16)
            return carry

        lax.fori_loop(0, count, place, 0)

    @pl.when(at_tile == 0)
    def _():
        unpack(row_ref, left, False)
        unpack(col_ref, right, True)

    lhs = left[:, pl.ds(pl.multiple_of(at_tile * tile, tile), tile)]
    width = right.shape[1]
    step = math.gcd(width, 1024)
    for at in range(0, width, step):
        out_ref[0, :, at : at + step] = lax.dot_general(
            lhs, right[:, at : at + step], (((0,), (0,)), ((), ())), preferred_element_type=jnp.float32
        )


def chi_block(row_panel, col_panel, weights, count, row_block, col_block):
    sources = weights.shape[0] // (FREQS * WEIGHT_ROWS)
    tile = math.gcd(row_block, 256)
    whole = lambda x: pl.BlockSpec(x.shape, lambda m: (0, 0), pipeline_mode=pl.Buffered(1))
    pairs = sources * count
    return pl.pallas_call(
        functools.partial(chi_kernel, count, tile),
        out_shape=jax.ShapeDtypeStruct((1, row_block, col_block), jnp.float32),
        grid=(row_block // tile,),
        in_specs=[whole(row_panel), whole(col_panel), whole(weights)],
        out_specs=pl.BlockSpec((1, tile, col_block), lambda m: (0, m, 0)),
        scratch_shapes=[
            pltpu.VMEM((max(row_panel.shape[0], col_panel.shape[0]), LANES), jnp.float32),
            pltpu.VMEM((pairs, row_block), jnp.bfloat16),
            pltpu.VMEM((pairs, col_block), jnp.bfloat16),
        ],
        compiler_params=pltpu.CompilerParams(vmem_limit_bytes=56 * 2**20),
        name="chi_block",
    )(row_panel, col_panel, weights)


def per_device(
    valence_orbitals,
    conduction_orbitals,
    valence_energy,
    conduction_energy,
    coulomb_root,
    pair_bands,
    slot_counts,
):
    grow_size = lax.axis_size("grow")
    gcol_size = lax.axis_size("gcol")
    factor = 1.0 / math.sqrt(2 * grow_size * gcol_size * SLOTS)
    half_slots = pair_bands.shape[1] // 2
    swap = [(0, 1), (1, 0)]

    con_own = conduction_orbitals.reshape(-1, M1, M2 * M3)
    con_other = lax.ppermute(con_own, "band", swap)
    own = jnp.concatenate([pair_bands.reshape(-1), slot_counts])
    other = lax.ppermute(own, "band", swap)
    band = lax.axis_index("band").astype(jnp.int32).reshape(1)
    density, weights = densities(
        valence_orbitals.reshape(-1, M1, M2 * M3), con_own, con_other, coulomb_root,
        own, other, band, valence_energy, conduction_energy, factor,
    )

    row_block = N1 * N2 * N3 // grow_size
    col_block = N1 * N2 * N3 // gcol_size

    def wire(blocks, block):
        parts = density.reshape(half_slots, blocks, block // LANES, LANES).transpose(1, 0, 2, 3)
        return parts.reshape(blocks, half_slots * (block // LANES), LANES)

    row_panel, col_panel, all_weights = exchange(
        wire(grow_size, row_block), wire(gcol_size, col_block), weights, grow_size, gcol_size
    )
    return chi_block(
        row_panel.reshape(-1, LANES),
        col_panel.reshape(-1, LANES),
        all_weights.reshape(-1, LANES),
        half_slots,
        row_block,
        col_block,
    )


def solution(mesh):
    return jax.shard_map(
        per_device,
        mesh=mesh,
        in_specs=(
            P(),
            P(("band", "grow", "gcol"), None),
            P(),
            P(),
            P(),
            P(None, ("band", "grow", "gcol")),
            P(("band", "grow", "gcol")),
        ),
        out_specs=P("band", "grow", "gcol"),
        check_vma=False,
    )
```

time: 145 us -> 75.4 us (0.52)
  the two profiles are of different devices: /device:TPU:11 before, /device:TPU:9 now
where the time goes in v2:
time: 75.4 us; the launch traced here: 75.2 us
  Pallas kernels  65.3 us (87%)
  local copies, waits for them, and re-layouts  8.27 us (11%)
  between operations  0.77 us (1%)
    pallas_call x1, Pallas kernels, exchange(): pl.pallas_call(functools.partial(exchange_kernel, grow, gcol), out_shape=...  39.4 us
    pallas_call x1, Pallas kernels, chi_block(): pl.pallas_call(functools.partial(chi_kernel, count, tile), out_shape=jax....  22.8 us
    unnamed x12, local copies, waits for them, and re-layouts  5.75 us
    pallas_call x1, Pallas kernels, densities(): pl.pallas_call(functools.partial(density_kernel, count, held_con, factor)...  3.05 us
  transfers between devices with their start and end apart: 2, of which 0 were waited for; matrix products, arithmetic and copies ran while one was open for 7% of the time, Pallas kernels for 0%

profile of v2, /device:TPU:9, one launch (start us, length us, event | category | flops | bytes accessed | tf_op | source)
XLA Modules:
  0.0 75.2 jit_solution(5428457916901938947)
XLA Ops:
  0.0 1.4 %copy.14 = bf16[1,4,32,3072]{3,2,1,0:T(8,128)(2,1)S(1)} copy(bf16[1,4,32,3072]{3,1,2,0:T(4,128)(2,1)} %bitcast.21) | data formatting | bytes 1572864
  1.4 0.7 collective-permute-start.1
  2.8 0.8 %reshape.32 = s32[40]{0:T(128)S(1)} reshape(s32[2,20]{1,0:T(2,128)} %param.14) | data formatting | bytes 320 | tf_op jit(solution)/shard_map/reshape | solution.py:328
  3.5 0.1 pad_add_fusion.own
  3.6 0.0 collective-permute-start
  3.6 0.8 %reshape.36.root_ref = f32[16,768]{1,0:T(8,128)S(1)} reshape(f32[12288]{0:T(1024)} %param.13) | data formatting | bytes 98304 | tf_op jit(solution)/shard_map/reshape | solution.py:127
  4.4 0.0 copy-start
  4.4 0.0 copy-start.1
  4.5 0.0 copy-start.3
  4.5 0.0 copy-start.4
  4.5 3.8 %copy.11 = bf16[2,8,32,3072]{3,2,1,0:T(8,128)(2,1)S(1)} copy(bf16[2,8,32,3072]{3,1,2,0:T(8,128)(2,1)} %bitcast.16) | data formatting | bytes 6291456
  8.2 0.0 collective-permute-done.other
  8.3 0.0 collective-permute-done.1.other_ref
  8.3 0.0 copy-done
  8.3 0.0 copy-done.1
  8.3 0.0 copy-done.3
  8.3 0.0 copy-done.4
  8.3 3.1 %pair_density.1 = (bf16[10,16,768]{2,1,0:T(8,128)(2,1)S(1)}, f32[2,16,128]{2,1,0:T(8,128)S(1)}) custom-call(s32[41]{0:T(128)S(1)} %pad_add_fusion.own, s32[41]{0:T(128)S(1)} %collective-permute-done.other, s32[1]{0:T(128)} %bitcast.band, f32[16]{0:T(128)S(1)} %copy-done.3, f32[128]{0:T(128)S(1)} %copy-done.4, bf16[16,32,3072]{2,1,0:T(8,128)(2,1)S(1)} %bitcast.13, ...), custom_call_target="tpu_custom_call" | custom-call | tf_op jit(solution)/shard_map/pair_density/pallas_call | solution.py:99
  11.4 0.0 copy-start.2
  11.4 0.6 copy-done.2
  12.0 0.2 reshape.37
  12.2 0.7 copy.10
  12.9 39.4 %panel_exchange.1 = (bf16[2,4,4,240,128]{4,3,2,1,0:T(8,128)(2,1)}, bf16[2,4,4,240,128]{4,3,2,1,0:T(8,128)(2,1)}, f32[2,4,4,2,16,128]{5,4,3,2,1,0:T(8,128)}) custom-call(bf16[4,240,128]{2,1,0:T(8,128)(2,1)} %bitcast.17, bf16[4,240,128]{2,1,0:T(8,128)(2,1)} %bitcast.18, f32[2,16,128]{2,1,0:T(8,128)} %copy-done.2), custom_call_target="tpu_custom_call" | custom-call | tf_op jit(solution)/shard_map/panel_exchange/pallas_call | solution.py:226
  52.4 22.8 %chi_block.1 = f32[1,3072,3072]{2,1,0:T(8,128)} custom-call(bf16[7680,128]{1,0:T(8,128)(2,1)} %bitcast.19, bf16[7680,128]{1,0:T(8,128)(2,1)} %bitcast.20, f32[1024,128]{1,0:T(8,128)} %bitcast.22), custom_call_target="tpu_custom_call" | custom-call | tf_op jit(solution)/shard_map/chi_block/pallas_call | solution.py:295
Async XLA Ops:
  1.4 6.9 %collective-permute-start.1 = (bf16[4,32,3072]{2,1,0:T(8,128)(2,1)S(1)}, bf16[4,32,3072]{2,1,0:T(8,128)(2,1)S(1)}, u32[]{:S(2)}, u32[]{:S(2)}) collective-permute-start(bf16[4,32,3072]{2,1,0:T(8,128)(2,1)S(1)} %bitcast.14), channel_id=1, source_target_pairs={{0,16},{16,0},{1,17},{17,1},{2,18},{18,2},{3,19},{19,3},{4,20},{20... | collective-permute-start | bytes 2359304 | tf_op jit(solution)/shard_map/ppermute | solution.py:327
  3.6 4.6 %collective-permute-start = (s32[41]{0:T(128)S(1)}, s32[41]{0:T(128)S(1)}, u32[]{:S(2)}, u32[]{:S(2)}) collective-permute-start(s32[41]{0:T(128)S(1)} %pad_add_fusion.own), channel_id=1, source_target_pairs={{0,16},{16,0},{1,17},{17,1},{2,18},{18,2},{3,19},{19,3},{4,20},{20... | collective-permute-start | bytes 500 | tf_op jit(solution)/shard_map/ppermute | solution.py:329
  4.4 3.8 %copy-start = (bf16[3072,768]{1,0:T(8,128)(2,1)S(1)}, bf16[3072,768]{1,0:T(8,128)(2,1)}, u32[]{:S(2)}) copy-start(bf16[3072,768]{1,0:T(8,128)(2,1)} %constant.11.clone.rest_ref) | copy-start | bytes 14155780
  4.4 3.8 %copy-start.1 = (bf16[160,320]{1,0:T(8,128)(2,1)S(1)}, bf16[160,320]{1,0:T(8,128)(2,1)}, u32[]{:S(2)}) copy-start(bf16[160,320]{1,0:T(8,128)(2,1)} %constant.10.clone.first_ref) | copy-start | bytes 307204
  4.5 3.8 %copy-start.3 = (f32[16]{0:T(128)S(1)}, f32[16]{0:T(128)}, u32[]{:S(2)}) copy-start(f32[16]{0:T(128)} %val_energy.1) | copy-start | bytes 196
  4.5 3.8 %copy-start.4 = (f32[128]{0:T(128)S(1)}, f32[128]{0:T(128)}, u32[]{:S(2)}) copy-start(f32[128]{0:T(128)} %con_energy.1) | copy-start | bytes 1540
  11.4 0.6 copy-start.2

commit v3 on v2

--- a/solution.py
+++ b/solution.py
@@ -130,7 +130,8 @@
 
 def exchange_kernel(
     grow, gcol, rows_in, cols_in, weights_in, rows, cols, weights,
-    local_sem, r1s, r1r, c1s, c1r, r2s, r2r, c2s, c2r, r3s, r3r, c3s, c3r, w1s, w1r, w2s, w2r, w3s, w3r,
+    local_sem, r1s, r1r, c1s, c1r, r2s, r2r, up_s, up_r, down_s, down_r, r3s, r3r, c3s, c3r,
+    w1s, w1r, w2s, w2r, w3s, w3r,
 ):
     b = lax.axis_index("band")
     g = lax.axis_index("grow")
@@ -171,13 +172,51 @@
             device_id=sibling, device_id_type=MESH,
         ).wait_recv()
 
-    for i in range(1, gcol):
-        send(weights_in, weights.at[b, c, g], w1s.at[i], w1r.at[i], (b, g, near_c[i]))
+    on_right = g + 1 < grow
+    on_left = g > 0
+    guarded = []
+
+    def send_if(condition, src, dst, send_sem, recv_sem, target):
+        copy = pltpu.make_async_remote_copy(
+            src_ref=src, dst_ref=dst, send_sem=send_sem, recv_sem=recv_sem,
+            device_id=target, device_id_type=MESH,
+        )
+
+        @pl.when(condition)
+        def _():
+            copy.start()
+
+        guarded.append((condition, copy))
+
+    right = (b, jnp.minimum(g + 1, grow - 1), c)
+    left = (b, jnp.maximum(g - 1, 0), c)
+
+    def spread(src, owner, i):
+        dst = cols.at[b, owner, g]
+        send_if(on_right, src, dst, up_s.at[1, i], up_r.at[1, i], right)
+        send_if(on_left, src, dst, down_s.at[1, i], down_r.at[1, i], left)
+        send(src, dst, c3s.at[0, i], c3r.at[0, i], sibling)
+
+    for i in range(1, gcol):
         send(cols_in.at[near_c[i]], cols.at[b, c, g], c1s.at[i], c1r.at[i], (b, g, near_c[i]))
     for i in range(1, grow):
         send(rows_in.at[near_g[i]], rows.at[b, c, g], r1s.at[i], r1r.at[i], (b, near_g[i], c))
-
-    own_col.wait()
+    spread(cols_in.at[c], c, 0)
+    for i in range(1, gcol):
+        send(weights_in, weights.at[b, c, g], w1s.at[i], w1r.at[i], (b, g, near_c[i]))
+    for i in range(1, gcol):
+        piece = cols.at[b, back_c[i], g]
+        arrive(piece, c1s.at[i], c1r.at[i])
+        spread(piece, back_c[i], i)
+
+    own_row.wait()
+    for i in range(1, grow):
+        arrive(rows.at[b, c, back_g[i]], r1s.at[i], r1r.at[i])
+    block = rows.at[b, c]
+    for i in range(1, gcol):
+        send(block, block, r2s.at[i], r2r.at[i], (b, g, near_c[i]))
+    send(block, block, r3s.at[0], r3r.at[0], sibling)
+
     own_weight.wait()
     for i in range(1, gcol):
         arrive(weights.at[b, back_c[i], g], w1s.at[i], w1r.at[i])
@@ -185,44 +224,66 @@
     for i in range(1, grow):
         send(block, block, w2s.at[i], w2r.at[i], (b, near_g[i], c))
     send(block, block, w3s.at[0], w3r.at[0], sibling)
-    for i in range(1, gcol):
-        arrive(cols.at[b, back_c[i], g], c1s.at[i], c1r.at[i])
-    block = cols.at[b, :, g]
-    for i in range(1, grow):
-        send(block, block, c2s.at[i], c2r.at[i], (b, near_g[i], c))
-    send(block, block, c3s.at[0], c3r.at[0], sibling)
-
-    own_row.wait()
-    for i in range(1, grow):
-        arrive(rows.at[b, c, back_g[i]], r1s.at[i], r1r.at[i])
-    block = rows.at[b, c]
-    for i in range(1, gcol):
-        send(block, block, r2s.at[i], r2r.at[i], (b, g, near_c[i]))
-    send(block, block, r3s.at[0], r3r.at[0], sibling)
-
-    for i in range(1, gcol):
-        block = rows.at[b, back_c[i]]
-        arrive(block, r2s.at[i], r2r.at[i])
-        send(block, block, r3s.at[i], r3r.at[i], sibling)
+
+    def rows_to_sibling():
+        for i in range(1, gcol):
+            block = rows.at[b, back_c[i]]
+            arrive(block, r2s.at[i], r2r.at[i])
+            send(block, block, r3s.at[i], r3r.at[i], sibling)
+
+    for s in range(1, grow):
+        if s == grow - 1:
+            rows_to_sibling()
+        low = jnp.maximum(g - s, 0)
+        high = jnp.minimum(g + s, grow - 1)
+        for i in range(gcol):
+            for has, at, S, R, onward, target, half in (
+                (g >= s, low, up_s, up_r, on_right, right, 0),
+                (g + s < grow, high, down_s, down_r, on_left, left, 1),
+            ):
+                piece = cols.at[b, back_c[i], at]
+
+                @pl.when(has)
+                def _():
+                    arrive(piece, S.at[s, i], R.at[s, i])
+
+                if s + 1 < grow:
+                    send_if(
+                        jnp.logical_and(has, onward), piece, piece, S.at[s + 1, i], R.at[s + 1, i], target
+                    )
+                send_if(has, piece, piece, c3s.at[s + half * grow, i], c3r.at[s + half * grow, i], sibling)
+
     for i in range(1, grow):
         block = weights.at[b, :, back_g[i]]
         arrive(block, w2s.at[i], w2r.at[i])
         send(block, block, w3s.at[i], w3r.at[i], sibling)
-    for i in range(1, grow):
-        block = cols.at[b, :, back_g[i]]
-        arrive(block, c2s.at[i], c2r.at[i])
-        send(block, block, c3s.at[i], c3r.at[i], sibling)
     for i in range(gcol):
         arrive(rows.at[1 - b, back_c[i]], r3s.at[i], r3r.at[i])
+        arrive(cols.at[1 - b, back_c[i], g], c3s.at[0, i], c3r.at[0, i])
     for i in range(grow):
         arrive(weights.at[1 - b, :, back_g[i]], w3s.at[i], w3r.at[i])
-        arrive(cols.at[1 - b, :, back_g[i]], c3s.at[i], c3r.at[i])
+    for s in range(1, grow):
+        low = jnp.maximum(g - s, 0)
+        high = jnp.minimum(g + s, grow - 1)
+        for i in range(gcol):
+            for has, at, half in ((g >= s, low, 0), (g + s < grow, high, 1)):
+
+                @pl.when(has)
+                def _():
+                    arrive(cols.at[1 - b, back_c[i], at], c3s.at[s + half * grow, i], c3r.at[s + half * grow, i])
+
+    own_col.wait()
     for copy in sent:
         copy.wait_send()
+    for condition, copy in guarded:
+
+        @pl.when(condition)
+        def _():
+            copy.wait_send()
 
 
 def exchange(rows_in, cols_in, weights_in, grow, gcol):
-    sem = lambda n: pltpu.SemaphoreType.DMA((n,))
+    sem = lambda *n: pltpu.SemaphoreType.DMA(n)
     return pl.pallas_call(
         functools.partial(exchange_kernel, grow, gcol),
         out_shape=(
@@ -234,8 +295,8 @@
         out_specs=(pl.BlockSpec(memory_space=pl.ANY),) * 3,
         scratch_shapes=[sem(3)]
         + [sem(grow)] * 2 + [sem(gcol)] * 2
-        + [sem(gcol)] * 2 + [sem(grow)] * 2
-        + [sem(gcol)] * 2 + [sem(grow)] * 2
+        + [sem(gcol)] * 2 + [sem(grow, gcol)] * 4
+        + [sem(gcol)] * 2 + [sem(2 * grow, gcol)] * 2
         + [sem(gcol)] * 2 + [sem(grow)] * 2 + [sem(grow)] * 2,
         compiler_params=pltpu.CompilerParams(collective_id=0, has_side_effects=True),
         name="panel_exchange",
@@ -280,7 +341,7 @@
 
     lhs = left[:, pl.ds(pl.multiple_of(at_tile * tile, tile), tile)]
     width = right.shape[1]
-    step = math.gcd(width, 1024)
+    step = math.gcd(width, 512)
     for at in range(0, width, step):
         out_ref[0, :, at : at + step] = lax.dot_general(
             lhs, right[:, at : at + step], (((0,), (0,)), ((), ())), preferred_element_type=jnp.float32
@@ -289,7 +350,7 @@
 
 def chi_block(row_panel, col_panel, weights, count, row_block, col_block):
     sources = weights.shape[0] // (FREQS * WEIGHT_ROWS)
-    tile = math.gcd(row_block, 256)
+    tile = math.gcd(row_block, 512)
     whole = lambda x: pl.BlockSpec(x.shape, lambda m: (0, 0), pipeline_mode=pl.Buffered(1))
     pairs = sources * count
     return pl.pallas_call(

time: 75.4 us -> 69.7 us (0.924)
  the two profiles are of different devices: /device:TPU:9 before, /device:TPU:0 now
where the time goes in v3:
time: 69.7 us; the launch traced here: 69.5 us
  Pallas kernels  59.8 us (86%)
  local copies, waits for them, and re-layouts  8.26 us (12%)
  between operations  0.77 us (1%)
    pallas_call x1, Pallas kernels, exchange(): pl.pallas_call(functools.partial(exchange_kernel, grow, gcol), out_shape=...  35.3 us
    pallas_call x1, Pallas kernels, chi_block(): pl.pallas_call(functools.partial(chi_kernel, count, tile), out_shape=jax....  21.4 us
    unnamed x12, local copies, waits for them, and re-layouts  5.75 us
    pallas_call x1, Pallas kernels, densities(): pl.pallas_call(functools.partial(density_kernel, count, held_con, factor)...  3.05 us
  transfers between devices with their start and end apart: 2, of which 0 were waited for; matrix products, arithmetic and copies ran while one was open for 8% of the time, Pallas kernels for 0%

profile of v3, /device:TPU:0, one launch (start us, length us, event | category | flops | bytes accessed | tf_op | source)
XLA Modules:
  0.0 69.5 jit_solution(7455858784830036787)
XLA Ops:
  0.0 1.4 %copy.14 = bf16[1,4,32,3072]{3,2,1,0:T(8,128)(2,1)S(1)} copy(bf16[1,4,32,3072]{3,1,2,0:T(4,128)(2,1)} %bitcast.21) | data formatting | bytes 1572864
  1.4 0.5 collective-permute-start.1
  2.5 0.8 %reshape.32 = s32[40]{0:T(128)S(1)} reshape(s32[2,20]{1,0:T(2,128)} %param.14) | data formatting | bytes 320 | tf_op jit(solution)/shard_map/reshape | solution.py:389
  3.3 0.1 pad_add_fusion.own
  3.4 0.1 collective-permute-start
  3.4 0.8 %reshape.36.root_ref = f32[16,768]{1,0:T(8,128)S(1)} reshape(f32[12288]{0:T(1024)} %param.13) | data formatting | bytes 98304 | tf_op jit(solution)/shard_map/reshape | solution.py:127
  4.3 0.0 copy-start
  4.3 0.0 copy-start.1
  4.3 0.0 copy-start.3
  4.3 0.0 copy-start.4
  4.3 3.8 %copy.11 = bf16[2,8,32,3072]{3,2,1,0:T(8,128)(2,1)S(1)} copy(bf16[2,8,32,3072]{3,1,2,0:T(8,128)(2,1)} %bitcast.16) | data formatting | bytes 6291456
  8.1 0.0 collective-permute-done.other
  8.1 0.0 collective-permute-done.1.other_ref
  8.1 0.0 copy-done
  8.1 0.0 copy-done.1
  8.1 0.0 copy-done.3
  8.1 0.0 copy-done.4
  8.1 3.1 %pair_density.1 = (bf16[10,16,768]{2,1,0:T(8,128)(2,1)S(1)}, f32[2,16,128]{2,1,0:T(8,128)S(1)}) custom-call(s32[41]{0:T(128)S(1)} %pad_add_fusion.own, s32[41]{0:T(128)S(1)} %collective-permute-done.other, s32[1]{0:T(128)} %bitcast.band, f32[16]{0:T(128)S(1)} %copy-done.3, f32[128]{0:T(128)S(1)} %copy-done.4, bf16[16,32,3072]{2,1,0:T(8,128)(2,1)S(1)} %bitcast.13, ...), custom_call_target="tpu_custom_call" | custom-call | tf_op jit(solution)/shard_map/pair_density/pallas_call | solution.py:99
  11.2 0.0 copy-start.2
  11.2 0.6 copy-done.2
  11.8 0.2 reshape.37
  12.0 0.7 %copy.10 = bf16[10,4,24,128]{3,2,0,1:T(8,128)(2,1)} copy(bf16[10,4,24,128]{3,2,1,0:T(8,128)(2,1)S(1)} %reshape.37) | data formatting | bytes 491520 | tf_op jit(solution)/shard_map/reshape | solution.py:401
  12.7 35.3 %panel_exchange.1 = (bf16[2,4,4,240,128]{4,3,2,1,0:T(8,128)(2,1)}, bf16[2,4,4,240,128]{4,3,2,1,0:T(8,128)(2,1)}, f32[2,4,4,2,16,128]{5,4,3,2,1,0:T(8,128)}) custom-call(bf16[4,240,128]{2,1,0:T(8,128)(2,1)} %bitcast.17, bf16[4,240,128]{2,1,0:T(8,128)(2,1)} %bitcast.18, f32[2,16,128]{2,1,0:T(8,128)} %copy-done.2), custom_call_target="tpu_custom_call" | custom-call | tf_op jit(solution)/shard_map/panel_exchange/pallas_call | solution.py:287
  48.1 21.4 %chi_block.1 = f32[1,3072,3072]{2,1,0:T(8,128)} custom-call(bf16[7680,128]{1,0:T(8,128)(2,1)} %bitcast.19, bf16[7680,128]{1,0:T(8,128)(2,1)} %bitcast.20, f32[1024,128]{1,0:T(8,128)} %bitcast.22), custom_call_target="tpu_custom_call" | custom-call | tf_op jit(solution)/shard_map/chi_block/pallas_call | solution.py:356
Async XLA Ops:
  1.4 6.7 %collective-permute-start.1 = (bf16[4,32,3072]{2,1,0:T(8,128)(2,1)S(1)}, bf16[4,32,3072]{2,1,0:T(8,128)(2,1)S(1)}, u32[]{:S(2)}, u32[]{:S(2)}) collective-permute-start(bf16[4,32,3072]{2,1,0:T(8,128)(2,1)S(1)} %bitcast.14), channel_id=1, source_target_pairs={{0,16},{16,0},{1,17},{17,1},{2,18},{18,2},{3,19},{19,3},{4,20},{20... | collective-permute-start | bytes 2359304 | tf_op jit(solution)/shard_map/ppermute | solution.py:388
  3.4 4.7 %collective-permute-start = (s32[41]{0:T(128)S(1)}, s32[41]{0:T(128)S(1)}, u32[]{:S(2)}, u32[]{:S(2)}) collective-permute-start(s32[41]{0:T(128)S(1)} %pad_add_fusion.own), channel_id=1, source_target_pairs={{0,16},{16,0},{1,17},{17,1},{2,18},{18,2},{3,19},{19,3},{4,20},{20... | collective-permute-start | bytes 500 | tf_op jit(solution)/shard_map/ppermute | solution.py:390
  4.3 3.8 %copy-start = (bf16[3072,768]{1,0:T(8,128)(2,1)S(1)}, bf16[3072,768]{1,0:T(8,128)(2,1)}, u32[]{:S(2)}) copy-start(bf16[3072,768]{1,0:T(8,128)(2,1)} %constant.11.clone.rest_ref) | copy-start | bytes 14155780
  4.3 3.8 %copy-start.1 = (bf16[160,320]{1,0:T(8,128)(2,1)S(1)}, bf16[160,320]{1,0:T(8,128)(2,1)}, u32[]{:S(2)}) copy-start(bf16[160,320]{1,0:T(8,128)(2,1)} %constant.10.clone.first_ref) | copy-start | bytes 307204
  4.3 3.8 %copy-start.3 = (f32[16]{0:T(128)S(1)}, f32[16]{0:T(128)}, u32[]{:S(2)}) copy-start(f32[16]{0:T(128)} %val_energy.1) | copy-start | bytes 196
  4.3 3.8 %copy-start.4 = (f32[128]{0:T(128)S(1)}, f32[128]{0:T(128)}, u32[]{:S(2)}) copy-start(f32[128]{0:T(128)} %con_energy.1) | copy-start | bytes 1540
  11.2 0.6 copy-start.2

commit v4 on v3

--- a/solution.py
+++ b/solution.py
@@ -197,25 +197,17 @@
         send_if(on_left, src, dst, down_s.at[1, i], down_r.at[1, i], left)
         send(src, dst, c3s.at[0, i], c3r.at[0, i], sibling)
 
+    spread(cols_in.at[c], c, 0)
     for i in range(1, gcol):
         send(cols_in.at[near_c[i]], cols.at[b, c, g], c1s.at[i], c1r.at[i], (b, g, near_c[i]))
     for i in range(1, grow):
         send(rows_in.at[near_g[i]], rows.at[b, c, g], r1s.at[i], r1r.at[i], (b, near_g[i], c))
-    spread(cols_in.at[c], c, 0)
     for i in range(1, gcol):
         send(weights_in, weights.at[b, c, g], w1s.at[i], w1r.at[i], (b, g, near_c[i]))
     for i in range(1, gcol):
         piece = cols.at[b, back_c[i], g]
         arrive(piece, c1s.at[i], c1r.at[i])
         spread(piece, back_c[i], i)
-
-    own_row.wait()
-    for i in range(1, grow):
-        arrive(rows.at[b, c, back_g[i]], r1s.at[i], r1r.at[i])
-    block = rows.at[b, c]
-    for i in range(1, gcol):
-        send(block, block, r2s.at[i], r2r.at[i], (b, g, near_c[i]))
-    send(block, block, r3s.at[0], r3r.at[0], sibling)
 
     own_weight.wait()
     for i in range(1, gcol):
@@ -225,6 +217,15 @@
         send(block, block, w2s.at[i], w2r.at[i], (b, near_g[i], c))
     send(block, block, w3s.at[0], w3r.at[0], sibling)
 
+    def rows_across():
+        own_row.wait()
+        for i in range(1, grow):
+            arrive(rows.at[b, c, back_g[i]], r1s.at[i], r1r.at[i])
+        block = rows.at[b, c]
+        for i in range(1, gcol):
+            send(block, block, r2s.at[i], r2r.at[i], (b, g, near_c[i]))
+        send(block, block, r3s.at[0], r3r.at[0], sibling)
+
     def rows_to_sibling():
         for i in range(1, gcol):
             block = rows.at[b, back_c[i]]
@@ -237,6 +238,8 @@
         low = jnp.maximum(g - s, 0)
         high = jnp.minimum(g + s, grow - 1)
         for i in range(gcol):
+            if s == 1 and i == 1:
+                rows_across()
             for has, at, S, R, onward, target, half in (
                 (g >= s, low, up_s, up_r, on_right, right, 0),
                 (g + s < grow, high, down_s, down_r, on_left, left, 1),

time: 69.7 us -> 69.7 us (level)
  no operation moved by 1% of the time
where the time goes in v4:
time: 69.7 us; the launch traced here: 69.5 us
  Pallas kernels  59.8 us (86%)
  local copies, waits for them, and re-layouts  8.26 us (12%)
  between operations  0.77 us (1%)
    pallas_call x1, Pallas kernels, exchange(): pl.pallas_call(functools.partial(exchange_kernel, grow, gcol), out_shape=...  35.4 us
    pallas_call x1, Pallas kernels, chi_block(): pl.pallas_call(functools.partial(chi_kernel, count, tile), out_shape=jax....  21.4 us
    unnamed x12, local copies, waits for them, and re-layouts  5.75 us
    pallas_call x1, Pallas kernels, densities(): pl.pallas_call(functools.partial(density_kernel, count, held_con, factor)...  3 us
  transfers between devices with their start and end apart: 2, of which 0 were waited for; matrix products, arithmetic and copies ran while one was open for 8% of the time, Pallas kernels for 0%

profile of v4, /device:TPU:0, one launch (start us, length us, event | category | flops | bytes accessed | tf_op | source)
XLA Modules:
  0.0 69.5 jit_solution(10442275400296055327)
XLA Ops:
  0.0 1.4 %copy.14 = bf16[1,4,32,3072]{3,2,1,0:T(8,128)(2,1)S(1)} copy(bf16[1,4,32,3072]{3,1,2,0:T(4,128)(2,1)} %bitcast.21) | data formatting | bytes 1572864
  1.4 0.5 collective-permute-start.1
  2.5 0.8 %reshape.32 = s32[40]{0:T(128)S(1)} reshape(s32[2,20]{1,0:T(2,128)} %param.14) | data formatting | bytes 320 | tf_op jit(solution)/shard_map/reshape | solution.py:392
  3.3 0.1 pad_add_fusion.own
  3.4 0.1 collective-permute-start
  3.4 0.8 %reshape.36.root_ref = f32[16,768]{1,0:T(8,128)S(1)} reshape(f32[12288]{0:T(1024)} %param.13) | data formatting | bytes 98304 | tf_op jit(solution)/shard_map/reshape | solution.py:127
  4.3 0.0 copy-start
  4.3 0.0 copy-start.1
  4.3 0.0 copy-start.3
  4.3 0.0 copy-start.4
  4.3 3.8 %copy.11 = bf16[2,8,32,3072]{3,2,1,0:T(8,128)(2,1)S(1)} copy(bf16[2,8,32,3072]{3,1,2,0:T(8,128)(2,1)} %bitcast.16) | data formatting | bytes 6291456
  8.1 0.0 collective-permute-done.other
  8.1 0.0 collective-permute-done.1.other_ref
  8.1 0.0 copy-done
  8.1 0.0 copy-done.1
  8.1 0.0 copy-done.3
  8.1 0.0 copy-done.4
  8.1 3.0 %pair_density.1 = (bf16[10,16,768]{2,1,0:T(8,128)(2,1)S(1)}, f32[2,16,128]{2,1,0:T(8,128)S(1)}) custom-call(s32[41]{0:T(128)S(1)} %pad_add_fusion.own, s32[41]{0:T(128)S(1)} %collective-permute-done.other, s32[1]{0:T(128)} %bitcast.band, f32[16]{0:T(128)S(1)} %copy-done.3, f32[128]{0:T(128)S(1)} %copy-done.4, bf16[16,32,3072]{2,1,0:T(8,128)(2,1)S(1)} %bitcast.13, ...), custom_call_target="tpu_custom_call" | custom-call | tf_op jit(solution)/shard_map/pair_density/pallas_call | solution.py:99
  11.1 0.0 copy-start.2
  11.1 0.6 copy-done.2
  11.7 0.2 reshape.37
  12.0 0.7 %copy.10 = bf16[10,4,24,128]{3,2,0,1:T(8,128)(2,1)} copy(bf16[10,4,24,128]{3,2,1,0:T(8,128)(2,1)S(1)} %reshape.37) | data formatting | bytes 491520 | tf_op jit(solution)/shard_map/reshape | solution.py:404
  12.7 35.4 %panel_exchange.1 = (bf16[2,4,4,240,128]{4,3,2,1,0:T(8,128)(2,1)}, bf16[2,4,4,240,128]{4,3,2,1,0:T(8,128)(2,1)}, f32[2,4,4,2,16,128]{5,4,3,2,1,0:T(8,128)}) custom-call(bf16[4,240,128]{2,1,0:T(8,128)(2,1)} %bitcast.17, bf16[4,240,128]{2,1,0:T(8,128)(2,1)} %bitcast.18, f32[2,16,128]{2,1,0:T(8,128)} %copy-done.2), custom_call_target="tpu_custom_call" | custom-call | tf_op jit(solution)/shard_map/panel_exchange/pallas_call | solution.py:290
  48.1 21.4 %chi_block.1 = f32[1,3072,3072]{2,1,0:T(8,128)} custom-call(bf16[7680,128]{1,0:T(8,128)(2,1)} %bitcast.19, bf16[7680,128]{1,0:T(8,128)(2,1)} %bitcast.20, f32[1024,128]{1,0:T(8,128)} %bitcast.22), custom_call_target="tpu_custom_call" | custom-call | tf_op jit(solution)/shard_map/chi_block/pallas_call | solution.py:359
Async XLA Ops:
  1.4 6.7 %collective-permute-start.1 = (bf16[4,32,3072]{2,1,0:T(8,128)(2,1)S(1)}, bf16[4,32,3072]{2,1,0:T(8,128)(2,1)S(1)}, u32[]{:S(2)}, u32[]{:S(2)}) collective-permute-start(bf16[4,32,3072]{2,1,0:T(8,128)(2,1)S(1)} %bitcast.14), channel_id=1, source_target_pairs={{0,16},{16,0},{1,17},{17,1},{2,18},{18,2},{3,19},{19,3},{4,20},{20... | collective-permute-start | bytes 2359304 | tf_op jit(solution)/shard_map/ppermute | solution.py:391
  3.4 4.7 %collective-permute-start = (s32[41]{0:T(128)S(1)}, s32[41]{0:T(128)S(1)}, u32[]{:S(2)}, u32[]{:S(2)}) collective-permute-start(s32[41]{0:T(128)S(1)} %pad_add_fusion.own), channel_id=1, source_target_pairs={{0,16},{16,0},{1,17},{17,1},{2,18},{18,2},{3,19},{19,3},{4,20},{20... | collective-permute-start | bytes 500 | tf_op jit(solution)/shard_map/ppermute | solution.py:393
  4.3 3.8 %copy-start = (bf16[3072,768]{1,0:T(8,128)(2,1)S(1)}, bf16[3072,768]{1,0:T(8,128)(2,1)}, u32[]{:S(2)}) copy-start(bf16[3072,768]{1,0:T(8,128)(2,1)} %constant.11.clone.rest_ref) | copy-start | bytes 14155780
  4.3 3.8 %copy-start.1 = (bf16[160,320]{1,0:T(8,128)(2,1)S(1)}, bf16[160,320]{1,0:T(8,128)(2,1)}, u32[]{:S(2)}) copy-start(bf16[160,320]{1,0:T(8,128)(2,1)} %constant.10.clone.first_ref) | copy-start | bytes 307204
  4.3 3.8 %copy-start.3 = (f32[16]{0:T(128)S(1)}, f32[16]{0:T(128)}, u32[]{:S(2)}) copy-start(f32[16]{0:T(128)} %val_energy.1) | copy-start | bytes 196
  4.3 3.8 %copy-start.4 = (f32[128]{0:T(128)S(1)}, f32[128]{0:T(128)}, u32[]{:S(2)}) copy-start(f32[128]{0:T(128)} %con_energy.1) | copy-start | bytes 1540
  11.1 0.6 copy-start.2
